TPU v7x, 512 devices: a whole 4x4x16 slice. The times are simulated.
512 devices in a mesh: dp: 16 (over y_hi, x, core), expert: 32 (over z, y_lo).
Axes of the slice: x: 4, y: 4 (y_hi: 2, y_lo: 2; y = y_hi * 2 + y_lo), z: 16, core: 2. Of those that a mesh axis runs over, the one named last changes fastest.
Arguments:
- grad_rows: bfloat16 [16, 256, 16, 3584], P('dp', 'expert'), may hold values from -6 to 6
- router_weight: float32 [16, 256, 16], P('dp', 'expert'), may hold values from 0.05 to 0.6
- send_counts: int32 [16, 256], P('dp', 'expert'), may hold values from 1 to 16, as said below
- gate_stash: bfloat16 [16, 512, 8192], P('dp', None, 'expert'), may hold values from -6 to 6
- up_stash: bfloat16 [16, 512, 8192], P('dp', None, 'expert'), may hold values from -6 to 6
- master_weight: float32 [3584, 8192], P('dp', 'expert'), may hold values from -0.1875 to 0.1875
- first_moment: float32 [3584, 8192], P('dp', 'expert'), may hold values from -18 to 18
- second_moment: float32 [3584, 8192], P('dp', 'expert'), may hold values from 10 to 100
Outputs:
- d_gate: bfloat16 [16, 512, 8192], P('dp', None, 'expert')
- d_up: bfloat16 [16, 512, 8192], P('dp', None, 'expert')
- new_master: float32 [3584, 8192], P('dp', 'expert')
- new_first: float32 [3584, 8192], P('dp', 'expert')
- new_second: float32 [3584, 8192], P('dp', 'expert')
- fresh_weight: bfloat16 [3584, 8192], P(None, 'expert')
Inputs may be any that keep to these rules, and one draw needn't show every extreme that they name: `send_counts`: in every replica one expert in flight receives exactly 16 rows from every source; the other counts are at most 8.
All inputs are finite; a program needn't handle non-finite values.
Results may differ from a plain program's by a relative error of at most 0.009.
Values may be sent and summed in bfloat16 or wider, within the bound.
A program may use at most 64 MiB of HBM per device.

v0:
```python
import jax
import jax.numpy as jnp
from jax import lax
from jax.sharding import PartitionSpec as P

WAYS = 4


learning_rate = 0.01
beta_one = 0.9
beta_two = 0.95
decay_rate = 0.1
epsilon = 1e-08


def local(
    grad_rows,
    router_weight,
    send_counts,
    gate_stash,
    up_stash,
    master_weight,
    first_moment,
    second_moment,
):
    slot_count = grad_rows.shape[2]
    width = grad_rows.shape[3]
    sources = lax.axis_size("expert")
    slots = jnp.arange(slot_count, dtype=jnp.int32)
    live = slots[None, :] < send_counts[0][:, None]
    scaled = jnp.where(
        live[..., None],
        router_weight[0][..., None] * grad_rows[0].astype(jnp.float32),
        jnp.float32(0.0),
    )
    scaled = scaled.astype(jnp.bfloat16)
    spread = jnp.repeat(scaled, WAYS, axis=0)
    gathered = lax.all_to_all(spread, "expert", split_axis=0, concat_axis=0, tiled=True).reshape(
        sources * slot_count, width
    )
    gate = gate_stash[0].astype(jnp.float32)
    up = up_stash[0].astype(jnp.float32)
    sigmoid_gate = jax.nn.sigmoid(gate)
    activated = gate * sigmoid_gate
    hidden = (activated * up).astype(jnp.bfloat16)
    columns = gathered
    d_hidden = jnp.dot(
        columns,
        lax.all_gather(master_weight.astype(jnp.bfloat16), "dp", axis=0, tiled=True),
        preferred_element_type=jnp.float32,
    )
    grad_gate = (d_hidden * up * sigmoid_gate * (1.0 + gate * (1.0 - sigmoid_gate))).astype(
        jnp.bfloat16
    )
    grad_up = (d_hidden * activated).astype(jnp.bfloat16)
    columns = gathered
    gradient = lax.psum_scatter(
        lax.dot_general(
            columns, hidden, (((0,), (0,)), ((), ())), preferred_element_type=jnp.float32
        ).astype(jnp.bfloat16),
        "dp",
        scatter_dimension=0,
        tiled=True,
    ).astype(jnp.float32)
    moment_a = beta_one * first_moment + (1.0 - beta_one) * gradient
    moment_b = beta_two * second_moment + (1.0 - beta_two) * gradient * gradient
    step_size = (
        moment_a / (1.0 - beta_one**5) / (jnp.sqrt(moment_b / (1.0 - beta_two**5)) + epsilon)
    )
    updated = master_weight - learning_rate * (step_size + decay_rate * master_weight)
    fresh = lax.all_gather(updated.astype(jnp.bfloat16), "dp", axis=0, tiled=True)
    return (grad_gate[None], grad_up[None], updated, moment_a, moment_b, fresh)


def solution(mesh):
    placed = (
        P("dp", "expert", None, None),
        P("dp", "expert", None),
        P("dp", "expert"),
        P("dp", None, "expert"),
        P("dp", None, "expert"),
        P("dp", "expert"),
        P("dp", "expert"),
        P("dp", "expert"),
    )
    return jax.shard_map(
        local,
        mesh=mesh,
        in_specs=placed,
        out_specs=(
            P("dp", None, "expert"),
            P("dp", None, "expert"),
            P("dp", "expert"),
            P("dp", "expert"),
            P("dp", "expert"),
            P(None, "expert"),
        ),
        check_vma=False,
    )
```

profile of v0, /device:TPU:1, one launch (start us, length us, event | category | flops | bytes accessed | tf_op | source)
XLA Modules:
  0.0 427.1 jit_solution(7074308684738614783)
XLA Ops:
  7.2 0.0 reduce-scatter.2.cloned.1.call-start
  7.2 0.7 iota_compare_fusion
  7.9 1.5 fusion.1
  9.4 0.4 broadcast_in_dim.25
  9.9 0.0 copy-start.4
  9.9 0.0 copy-start.5
  9.9 182.6 %all_to_all.5 = bf16[32,16,3584]{2,1,0:T(8,128)(2,1)S(1)} all-to-all(bf16[32,16,3584]{2,1,0:T(8,128)(2,1)S(1)} %bitcast.59), channel_id=1, replica_groups=mesh['dp'=16,'expert'=32] {'expert'}, dimensions={0} | all-to-all | bytes 7340032 | tf_op jit(solution)/shard_map/all_to_all | solution.py:38
  192.5 0.0 copy-start
  192.5 1.8 copy-done
  194.3 0.0 copy-done.4
  194.3 0.0 copy-done.5
  194.3 2.5 convolution_convert_fusion
  196.8 0.0 copy-start.1
  196.8 0.0 copy-start.2
  196.8 0.0 copy-start.3
  196.8 0.0 reduce-scatter.2.cloned.1.call-update
  196.9 0.0 all-gather.3.cloned.1.call-start
  196.9 85.5 %reduce-scatter.2.cloned.1.call-done = bf16[224,256]{1,0:T(8,128)(2,1)} async-done(((bf16[3584,256]{1,0:T(8,128)(2,1)}), bf16[224,256]{1,0:T(8,128)(2,1)}) %reduce-scatter.2.cloned.1.call-update) | async-done | bytes 114704 | tf_op jit(solution)/shard_map/reduce_scatter | solution.py:57
  282.4 0.0 copy-done.1
  282.4 0.0 copy-done.2
  282.4 0.0 copy-done.3
  282.4 1.9 fusion.26
  284.4 0.0 all-gather.3.cloned.1.call-update
  284.4 0.0 all-gather.5.cloned.1.call-start
  284.4 0.7 all-gather.5.cloned.1.call-update
  285.1 66.2 %all-gather.3.cloned.1.call-done = bf16[3584,256]{1,0:T(8,128)(2,1)} async-done(((bf16[224,256]{1,0:T(8,128)(2,1)}), bf16[3584,256]{1,0:T(8,128)(2,1)}) %all-gather.3.cloned.1.call-update) | async-done | bytes 1835024 | tf_op jit(solution)/shard_map/all_gather | solution.py:49
  351.3 4.6 %fusion.21 = (bf16[1,512,256]{2,1,0:T(8,128)(2,1)}, bf16[1,512,256]{2,1,0:T(8,128)(2,1)}) fusion(bf16[1,512,256]{2,1,0:T(8,128)(2,1)S(1)} %copy-done.4, bf16[1,512,256]{2,1,0:T(8,128)(2,1)S(1)} %copy-done.5, bf16[512,3584]{1,0:T(8,128)(2,1)} %bitcast.61, bf16[3584,256]{1,0:T(8,128)(2,1)} %all-gather.3.cloned.1.call-done), kind=kOutput, calls=%fused_computation.29 | convolution fusion | flops 941490176 | bytes 6553600 | tf_op jit(solution)/shard_map/dot_general | solution.py:47
  355.9 61.8 %all-gather.5.cloned.1.call-done = bf16[3584,256]{1,0:T(8,128)(2,1)} async-done(((bf16[224,256]{1,0:T(8,128)(2,1)}), bf16[3584,256]{1,0:T(8,128)(2,1)}) %all-gather.5.cloned.1.call-update) | async-done | bytes 1835024 | tf_op jit(solution)/shard_map/all_gather | solution.py:71
  417.7 2.8 copy.15
Async XLA Ops:
  7.2 275.3 %reduce-scatter.2.cloned.1.call-start = ((), (), s32[]{:S(2)}) async-start(), calls=%async_computation.3 | async-start | bytes 1949696 | tf_op jit(solution)/shard_map/reduce_scatter | solution.py:57
  9.9 184.4 %copy-start.4 = (bf16[1,512,256]{2,1,0:T(8,128)(2,1)S(1)}, bf16[1,512,256]{2,1,0:T(8,128)(2,1)}, u32[]{:S(2)}) copy-start(bf16[1,512,256]{2,1,0:T(8,128)(2,1)} %param.11) | copy-start | bytes 786436
  9.9 184.4 %copy-start.5 = (bf16[1,512,256]{2,1,0:T(8,128)(2,1)S(1)}, bf16[1,512,256]{2,1,0:T(8,128)(2,1)}, u32[]{:S(2)}) copy-start(bf16[1,512,256]{2,1,0:T(8,128)(2,1)} %param.12) | copy-start | bytes 786436
  192.5 1.8 copy-start
  196.8 85.6 %copy-start.1 = (f32[224,256]{1,0:T(8,128)S(1)}, f32[224,256]{1,0:T(8,128)}, u32[]{:S(2)}) copy-start(f32[224,256]{1,0:T(8,128)} %param.13) | copy-start | bytes 688132
  196.8 85.6 %copy-start.2 = (f32[224,256]{1,0:T(8,128)S(1)}, f32[224,256]{1,0:T(8,128)}, u32[]{:S(2)}) copy-start(f32[224,256]{1,0:T(8,128)} %param.14) | copy-start | bytes 688132
  196.8 85.6 %copy-start.3 = (f32[224,256]{1,0:T(8,128)S(1)}, f32[224,256]{1,0:T(8,128)}, u32[]{:S(2)}) copy-start(f32[224,256]{1,0:T(8,128)} %param.15) | copy-start | bytes 688132
  196.9 154.5 %all-gather.3.cloned.1.call-start = ((), (), s32[]{:S(2)}) async-start(), calls=%async_computation.2 | async-start | bytes 1949696 | tf_op jit(solution)/shard_map/all_gather | solution.py:49
  284.4 133.3 %all-gather.5.cloned.1.call-start = ((), (), s32[]{:S(2)}) async-start(), calls=%async_computation.4 | async-start | bytes 1949696 | tf_op jit(solution)/shard_map/all_gather | solution.py:71
Sparse Core Ops, SparseCore 0:
  197.0 85.4 reduce-scatter.1
  286.8 64.4 all-gather.2
  355.7 61.9 all-gather.4
where the time goes:
time: 427 us
  waiting for transfers between devices  214 us (50%)
  blocking collectives  183 us (43%)
  between operations  13.8 us (3%)
  matrix products  7.1 us (2%)
  local copies, waits for them, and re-layouts  5.1 us (1%)
    all_to_all x1, blocking collectives, local(): lax.all_to_all(spread, 'expert', split_axis=0, concat_axis=0, tiled=True)  183 us
    reduce_scatter x1, waiting for transfers between devices, local(): lax.psum_scatter(lax.dot_general(columns, hidden, (((0,), (0,)), ((), ())...  85.5 us
    all_gather x1, waiting for transfers between devices, local(): lax.all_gather(master_weight.astype(jnp.bfloat16), 'dp', axis=0, tiled=True)  66.2 us
    all_gather x1, waiting for transfers between devices, local(): lax.all_gather(updated.astype(jnp.bfloat16), 'dp', axis=0, tiled=True)  61.8 us
  transfers between devices with their start and end apart: 3, of which 3 were waited for; matrix products, arithmetic and copies ran while one was open for 1% of the time, Pallas kernels for 0%

commit v1 on v0

v1 whole, which is shorter than its diff:
```python
import functools

import jax
import jax.numpy as jnp
from jax import lax
from jax.experimental import pallas as pl
from jax.experimental.pallas import tpu as pltpu
from jax.sharding import PartitionSpec as P

UNITS = (2, 2, 2, 1)
STRIP = 32

learning_rate = 0.01
beta_one = 0.9
beta_two = 0.95
decay_rate = 0.1
epsilon = 1e-08

MESH = pl.DeviceIdType.MESH
BF16 = jnp.bfloat16
F32 = jnp.float32


def kernel(
    nx,
    nz,
    rows_ref,
    weight_ref,
    count_ref,
    gate_ref,
    up_ref,
    master_ref,
    first_ref,
    second_ref,
    dgate_ref,
    dup_ref,
    newm_ref,
    newf_ref,
    news_ref,
    fresh_ref,
    *scratch,
):
    chunks = len(UNITS)
    send, recv, part, gsend, grecv, summed, pieces = (
        scratch[k * chunks : (k + 1) * chunks] for k in range(7)
    )
    (
        wown,
        wfull,
        hid,
        total,
        dh_out,
        dh_in,
        send_s,
        recv_s,
        pass_s,
        ws_s,
        wr_s,
        wcs_s,
        wcr_s,
        pair_s,
        gs_s,
        gr_s,
        ps_s,
        pr_s,
        as_s,
        ar_s,
        cs_s,
        cr_s,
    ) = scratch[7 * chunks :]
    flight, slots, width = rows_ref.shape
    shard, cols = master_ref.shape
    half = width // 2
    near = nz // 2

    i, ez = lax.axis_index("dp"), lax.axis_index("expert")
    c, x, yh = lax.rem(i, 2), lax.rem(lax.div(i, 2), nx), lax.div(i, 2 * nx)
    z, yl = lax.div(ez, 2), lax.rem(ez, 2)
    zl = lax.rem(z, 2)
    sibling = {"dp": i + 1 - 2 * c}
    z_pair = {"expert": ez + 2 - 4 * zl}
    y_pair = {"expert": ez + 1 - 2 * yl}

    def dp_of(yh_, x_):
        return yh_ * (2 * nx) + x_ * 2 + c

    def remote(src, dst, s, r, to):
        return pltpu.make_async_remote_copy(
            src_ref=src, dst_ref=dst, send_sem=s, recv_sem=r, device_id=to, device_id_type=MESH
        )

    def source_z(zz, zzl, t):
        return lax.rem(zz + jnp.where(zzl == 0, nz - t, t), nz)

    barrier = pltpu.get_barrier_semaphore()

    def greet(to):
        pl.semaphore_signal(barrier, inc=1, device_id=to, device_id_type=MESH)

    greet(sibling)
    greet(z_pair)

    def greet_line(t, carry):
        zs = source_z(z, zl, t)
        for ys in range(2):

            @pl.when(jnp.logical_or(t != 0, yl != ys))
            def _():
                greet({"expert": zs * 2 + ys})

        return carry

    lax.fori_loop(0, near, greet_line, 0)

    def greet_plane(k, carry):
        yh_, x_ = lax.div(k, nx), lax.rem(k, nx)
        for ys in range(2):

            @pl.when(jnp.logical_or(dp_of(yh_, x_) != i, yl != ys))
            def _():
                greet({"dp": dp_of(yh_, x_), "expert": z * 2 + ys})

        return carry

    lax.fori_loop(0, 2 * nx, greet_plane, 0)

    lane = lax.broadcasted_iota(jnp.int32, (slots, 128), 1)
    group = lax.div(lane, STRIP)
    eye = lax.broadcasted_iota(jnp.int32, (slots, slots), 0) == lax.broadcasted_iota(
        jnp.int32, (slots, slots), 1
    )
    slot_of = lax.broadcasted_iota(jnp.int32, (slots, 1), 0)
    per_tile = 128 // STRIP

    def scale(e, carry):
        row = weight_ref[pl.ds(e, 1), :]
        factor = jnp.sum(
            jnp.where(eye, jnp.broadcast_to(row, (slots, slots)), 0.0), axis=1, keepdims=True
        )
        factor = jnp.where(slot_of < count_ref[0, e], factor, 0.0)
        scaled = rows_ref[e].astype(F32) * factor
        for h in range(2):
            start = 0
            for m, units in enumerate(UNITS):
                span = 2 * nx * units * STRIP
                for tile in range(span // 128):
                    out = None
                    for a in range(per_tile):
                        owner, strip = divmod(tile * per_tile + a, units)
                        at = h * half + owner * shard + (start + strip) * STRIP
                        base, off = at // 128 * 128, at % 128
                        moved = scaled[:, base : base + 128]
                        shift = (a * STRIP - off) % 128
                        if shift:
                            moved = pltpu.roll(moved, shift, 1)
                        out = moved if out is None else jnp.where(group == a, moved, out)
                    send[m][e, h, :, tile * 128 : (tile + 1) * 128] = out.astype(BF16)
                start += units
        return carry

    lax.fori_loop(0, flight, scale, 0)
    wown[...] = master_ref[...].astype(BF16)

    pl.semaphore_wait(barrier, 2 * near - 1 + 4 * nx - 1 + 2)

    def exchange(m):
        def one(k, carry):
            t = near - 1 - k
            up_way = lax.rem(z + t, 2) == 0
            zd = lax.rem(z + jnp.where(up_way, t, nz - t), nz)
            e = lax.div(zd, 2)
            for h in range(2):
                own = jnp.logical_and(t == 0, yl == h)

                @pl.when(jnp.logical_not(own))
                def _():
                    remote(
                        send[m].at[e, h],
                        recv[m].at[ez],
                        send_s.at[m, t, h],
                        recv_s.at[m, ez],
                        {"expert": zd * 2 + h},
                    ).start()

                @pl.when(own)
                def _():
                    pltpu.make_async_copy(
                        send[m].at[e, h], recv[m].at[ez], recv_s.at[m, ez]
                    ).start()

            return carry

        lax.fori_loop(0, near, one, 0)

    exchange(0)

    def spread_weights(k, carry):
        yh_, x_ = lax.div(k, nx), lax.rem(k, nx)
        to = dp_of(yh_, x_)
        slot = wfull.at[yl, x, c]
        own = jnp.logical_and(to == i, yl == yh)

        @pl.when(jnp.logical_not(own))
        def _():
            remote(
                wown, slot, ws_s.at[yh_, x_], wr_s.at[yl, x], {"dp": to, "expert": z * 2 + yh}
            ).start()

        @pl.when(own)
        def _():
            pltpu.make_async_copy(wown, slot, wr_s.at[yl, x]).start()

        return carry

    lax.fori_loop(0, 2 * nx, spread_weights, 0)
    for m in range(1, chunks):
        exchange(m)

    def swish(k, carry):
        at = pl.ds(pl.multiple_of(k * 128, 128), 128)
        gate = gate_ref[at, :].astype(F32)
        up = up_ref[at, :].astype(F32)
        hid[yl, at, :] = (gate * jax.nn.sigmoid(gate) * up).astype(BF16)
        return carry

    lax.fori_loop(0, gate_ref.shape[0] // 128, swish, 0)
    hid_copy = remote(hid.at[yl], hid.at[yl], pair_s.at[0], pair_s.at[1], y_pair)
    hid_copy.start()

    def pass_on(m):
        def one(k, carry):
            t = near - 1 - k
            for ys in range(2):
                s = source_z(z, zl, t) * 2 + ys
                copy = remote(
                    recv[m].at[s], recv[m].at[s], pass_s.at[m, t, ys], recv_s.at[m, s], z_pair
                )
                copy.wait_recv()
                copy.start()
            return carry

        lax.fori_loop(0, near, one, 0)

    def arrived(m):
        def one(k, carry):
            t = near - 1 - k
            for ys in range(2):
                s = source_z(z + 1 - 2 * zl, 1 - zl, t) * 2 + ys
                remote(
                    recv[m].at[s], recv[m].at[s], pass_s.at[m, t, ys], recv_s.at[m, s], z_pair
                ).wait_recv()
            return carry

        lax.fori_loop(0, near, one, 0)

    def weight_copy(k):
        yl_, x_ = lax.div(k, nx), lax.rem(k, nx)
        return yl_, x_, remote(
            wfull.at[yl_, x_, c],
            wfull.at[yl_, x_, c],
            wcs_s.at[yl_, x_],
            wcr_s.at[yl_, x_],
            sibling,
        )

    def weights_to_sibling(k, carry):
        yl_, x_, copy = weight_copy(k)
        remote(wown, wfull.at[yl_, x_, c], ws_s.at[0, 0], wr_s.at[yl_, x_], sibling).wait_recv()
        copy.start()
        return carry

    def weights_arrived(k, carry):
        weight_copy(k)[2].wait_recv()
        return carry

    starts = [sum(UNITS[:m]) * STRIP for m in range(chunks)]
    counts = [units * STRIP for units in UNITS]

    def to_sibling(m):
        return remote(gsend[m], grecv[m], gs_s.at[m], gr_s.at[m], sibling)

    def columns_of(m):
        return recv[m][...].reshape(recv[m].shape[0] * slots, recv[m].shape[2])

    def gradient(m):
        for y_ in range(2):
            part[m][y_] = lax.dot_general(
                columns_of(m), hid[y_], (((0,), (0,)), ((), ())), preferred_element_type=F32
            ).reshape(nx, 2, counts[m], cols)
        gsend[m][...] = part[m][:, :, 1 - c].astype(BF16)
        to_sibling(m).start()

    def back(m):
        for y_ in range(2):
            block = wfull[y_, :, :, starts[m] : starts[m] + counts[m], :].reshape(-1, cols)
            product = jnp.dot(columns_of(m), block, preferred_element_type=F32)
            if m:
                total[y_] += product
            else:
                total[y_] = product

    def piece_copy(m, k):
        y_, x_ = lax.div(k, nx), lax.rem(k, nx)
        to = dp_of(yl, x_)
        own = jnp.logical_and(to == i, yl == y_)
        src, dst, sem = summed[m].at[y_, x_], pieces[m].at[yh * nx + x], pr_s.at[m, yh * nx + x]
        return (
            own,
            remote(src, dst, ps_s.at[m, k], sem, {"dp": to, "expert": z * 2 + y_}),
            (src, dst, sem),
        )

    def reduce_pieces(m):
        to_sibling(m).wait_recv()
        summed[m][...] = (part[m][:, :, c] + grecv[m][...].astype(F32)).astype(BF16)

        def one(k, carry):
            own, copy, local = piece_copy(m, k)

            @pl.when(jnp.logical_not(own))
            def _():
                copy.start()

            @pl.when(own)
            def _():
                pltpu.make_async_copy(*local).start()

            return carry

        lax.fori_loop(0, 2 * nx, one, 0)

    def fresh_slot(m, k, core):
        return fresh_ref.at[k, core, starts[m] : starts[m] + counts[m]]

    def fresh_copy(m, k, source):
        return remote(
            fresh_slot(m, source, c),
            fresh_slot(m, source, c),
            as_s.at[m, k],
            ar_s.at[m, source],
            {"dp": k * 2 + c},
        )

    def update(m):
        def one(k, carry):
            remote(
                summed[m].at[0, 0], pieces[m].at[k], ps_s.at[m, k], pr_s.at[m, k], sibling
            ).wait_recv()
            return carry

        lax.fori_loop(0, 2 * nx, one, 0)
        at = slice(starts[m], starts[m] + counts[m])
        grad = jnp.sum(pieces[m][...].astype(F32), axis=0)
        master = master_ref[at, :]
        moment_a = beta_one * first_ref[at, :] + (1.0 - beta_one) * grad
        moment_b = beta_two * second_ref[at, :] + (1.0 - beta_two) * grad * grad
        step = (
            moment_a
            / (1.0 - beta_one**5)
            / (jnp.sqrt(moment_b / (1.0 - beta_two**5)) + epsilon)
        )
        updated = master - learning_rate * (step + decay_rate * master)
        newm_ref[at, :] = updated
        newf_ref[at, :] = moment_a
        news_ref[at, :] = moment_b
        me = yh * nx + x
        fresh_ref[me, c, at, :] = updated.astype(BF16)

        def send_one(k, carry):
            @pl.when(k != me)
            def _():
                fresh_copy(m, k, me).start()

            return carry

        lax.fori_loop(0, 2 * nx, send_one, 0)

    def fresh_to_sibling(m):
        at = pl.ds(starts[m], counts[m])
        return remote(
            fresh_ref.at[:, c, at], fresh_ref.at[:, c, at], cs_s.at[m], cr_s.at[m], sibling
        )

    def gather(m):
        me = yh * nx + x

        def one(k, carry):
            @pl.when(k != me)
            def _():
                fresh_copy(m, k, k).wait_recv()

            return carry

        lax.fori_loop(0, 2 * nx, one, 0)
        fresh_to_sibling(m).start()

    dh_copy = remote(dh_out, dh_in, pair_s.at[2], pair_s.at[3], y_pair)

    def finish_hidden():
        dh_copy.wait_recv()

        def one(k, carry):
            at = pl.ds(pl.multiple_of(k * 128, 128), 128)
            gate = gate_ref[at, :].astype(F32)
            up = up_ref[at, :].astype(F32)
            sig = jax.nn.sigmoid(gate)
            dh = total[yl, at, :] + dh_in[at, :].astype(F32)
            dgate_ref[at, :] = (dh * up * sig * (1.0 + gate * (1.0 - sig))).astype(BF16)
            dup_ref[at, :] = (dh * (gate * sig)).astype(BF16)
            return carry

        lax.fori_loop(0, gate_ref.shape[0] // 128, one, 0)

    pass_on(0)
    lax.fori_loop(0, 2 * nx, weights_to_sibling, 0)
    if chunks > 1:
        pass_on(1)
    hid_copy.wait_recv()
    for m in range(chunks):
        arrived(m)
        gradient(m)
        if m == 0:
            lax.fori_loop(0, 2 * nx, weights_arrived, 0)
        back(m)
        if m == chunks - 1:
            dh_out[...] = total[1 - yl].astype(BF16)
            dh_copy.start()
        reduce_pieces(m)
        if m >= 1:
            update(m - 1)
        if m + 2 < chunks:
            pass_on(m + 2)
        if m >= 2:
            gather(m - 2)
    update(chunks - 1)
    if chunks > 1:
        gather(chunks - 2)
    finish_hidden()
    gather(chunks - 1)

    for m in range(chunks):
        fresh_to_sibling(m).wait()
        to_sibling(m).wait_send()

        def sent(t, carry, m=m):
            for h in range(2):

                @pl.when(jnp.logical_or(t != 0, yl != h))
                def _():
                    remote(
                        send[m].at[0, h],
                        recv[m].at[0],
                        send_s.at[m, t, h],
                        recv_s.at[m, 0],
                        z_pair,
                    ).wait_send()

                remote(
                    recv[m].at[0], recv[m].at[0], pass_s.at[m, t, h], recv_s.at[m, 0], z_pair
                ).wait_send()
            return carry

        lax.fori_loop(0, near, sent, 0)

        def sent_plane(k, carry, m=m):
            own, copy, _ = piece_copy(m, k)

            @pl.when(jnp.logical_not(own))
            def _():
                copy.wait_send()

            @pl.when(k != yh * nx + x)
            def _():
                fresh_copy(m, k, k).wait_send()

            return carry

        lax.fori_loop(0, 2 * nx, sent_plane, 0)

    def sent_weights(k, carry):
        yh_, x_ = lax.div(k, nx), lax.rem(k, nx)

        @pl.when(jnp.logical_not(jnp.logical_and(dp_of(yh_, x_) == i, yl == yh)))
        def _():
            remote(
                wown, wfull.at[0, 0, 0], ws_s.at[yh_, x_], wr_s.at[0, 0], sibling
            ).wait_send()

        weight_copy(k)[2].wait_send()
        return carry

    lax.fori_loop(0, 2 * nx, sent_weights, 0)
    hid_copy.wait_send()
    dh_copy.wait_send()


def local(nx, nz, rows, weight, count, gate, up, master, first, second):
    _, flight, slots, width = rows.shape
    shard, cols = master.shape
    _, received, _ = gate.shape
    chunks = len(UNITS)
    counts = [units * STRIP for units in UNITS]
    assert sum(counts) == shard and cols % 128 == 0
    spans = [2 * nx * n for n in counts]
    vmem = pl.BlockSpec(memory_space=pltpu.VMEM)
    dma = pltpu.SemaphoreType.DMA
    near = nz // 2
    scratch = (
        [pltpu.VMEM((flight, 2, slots, n), BF16) for n in spans]
        + [pltpu.VMEM((2 * nz, slots, n), BF16) for n in spans]
        + [pltpu.VMEM((2, nx, 2, n, cols), F32) for n in counts]
        + [pltpu.VMEM((2, nx, n, cols), BF16) for n in counts]
        + [pltpu.VMEM((2, nx, n, cols), BF16) for n in counts]
        + [pltpu.VMEM((2, nx, n, cols), BF16) for n in counts]
        + [pltpu.VMEM((2 * nx, n, cols), BF16) for n in counts]
        + [
            pltpu.VMEM((shard, cols), BF16),
            pltpu.VMEM((2, nx, 2, shard, cols), BF16),
            pltpu.VMEM((2, received, cols), BF16),
            pltpu.VMEM((2, received, cols), F32),
            pltpu.VMEM((received, cols), BF16),
            pltpu.VMEM((received, cols), BF16),
            dma((chunks, near, 2)),
            dma((chunks, 2 * nz)),
            dma((chunks, near, 2)),
            dma((2, nx)),
            dma((2, nx)),
            dma((2, nx)),
            dma((2, nx)),
            dma((4,)),
            dma((chunks,)),
            dma((chunks,)),
            dma((chunks, 2 * nx)),
            dma((chunks, 2 * nx)),
            dma((chunks, 2 * nx)),
            dma((chunks, 2 * nx)),
            dma((chunks,)),
            dma((chunks,)),
        ]
    )
    outs = pl.pallas_call(
        functools.partial(kernel, nx, nz),
        out_shape=[
            jax.ShapeDtypeStruct((received, cols), BF16),
            jax.ShapeDtypeStruct((received, cols), BF16),
            jax.ShapeDtypeStruct((shard, cols), F32),
            jax.ShapeDtypeStruct((shard, cols), F32),
            jax.ShapeDtypeStruct((shard, cols), F32),
            jax.ShapeDtypeStruct((2 * nx, 2, shard, cols), BF16),
        ],
        in_specs=[vmem, vmem, pl.BlockSpec(memory_space=pltpu.SMEM)] + [vmem] * 5,
        out_specs=[vmem] * 6,
        scratch_shapes=scratch,
        compiler_params=pltpu.CompilerParams(
            collective_id=0, has_side_effects=True, vmem_limit_bytes=50 * 1024 * 1024
        ),
    )(rows[0], weight[0], count, gate[0], up[0], master, first, second)
    return (
        outs[0][None],
        outs[1][None],
        outs[2],
        outs[3],
        outs[4],
        outs[5].reshape(4 * nx * shard, cols),
    )


def solution(mesh):
    nx, nz = mesh.shape["dp"] // 4, mesh.shape["expert"] // 2
    placed = (
        P("dp", "expert", None, None),
        P("dp", "expert", None),
        P("dp", "expert"),
        P("dp", None, "expert"),
        P("dp", None, "expert"),
        P("dp", "expert"),
        P("dp", "expert"),
        P("dp", "expert"),
    )
    return jax.shard_map(
        functools.partial(local, nx, nz),
        mesh=mesh,
        in_specs=placed,
        out_specs=(
            P("dp", None, "expert"),
            P("dp", None, "expert"),
            P("dp", "expert"),
            P("dp", "expert"),
            P("dp", "expert"),
            P(None, "expert"),
        ),
        check_vma=False,
    )
```

time: 427 us -> 113 us (0.26)
  waiting for transfers between devices: 214 us -> 0 us
  blocking collectives: 183 us -> 0 us
  Pallas kernels: 0 us -> 100 us
  between operations: 13.8 us -> 0.67 us
  matrix products: 7.1 us -> 0 us
  local copies, waits for them, and re-layouts: 5.1 us -> 11.9 us
    all_to_all x1 -> x0, blocking collectives: 183 us -> none  [local(): lax.all_to_all(spread, 'expert', split_axis=0, concat_axis=0, tiled=True)]
    all_gather x2 -> x0, waiting for transfers between devices: 128 us -> none  [the longest x1 66.2 us: local(): lax.all_gather(master_weight.astype(jnp.bfloat16), 'dp', axis=0, tiled=True)]
    pallas_call x0 -> x1, Pallas kernels: none -> 100 us  [local(): pl.pallas_call(functools.partial(kernel, nx, nz), out_shape=[jax.ShapeDty...]
    reduce_scatter x1 -> x0, waiting for transfers between devices: 85.5 us -> none  [local(): lax.psum_scatter(lax.dot_general(columns, hidden, (((0,), (0,)), ((), ())...]
    unnamed x13 -> x24, local copies, waits for them, and re-layouts: 4.67 us -> 11.9 us
    dot_general x2 -> x0, matrix products: 7.1 us -> none  [the longest x1 4.59 us: local(): jnp.dot(columns, lax.all_gather(master_weight.astype(jnp.bfloat16), 'dp',...]
  transfers between devices with their start and end apart: 3 -> 0, of which waited for: 3 -> 0; matrix products, arithmetic and copies ran while one was open for 1% -> 0% of each run, Pallas kernels for 0% -> 0%
where the time goes in v1:
time: 113 us
  Pallas kernels  100 us (88%)
  local copies, waits for them, and re-layouts  11.9 us (11%)
    pallas_call x1, Pallas kernels, local(): pl.pallas_call(functools.partial(kernel, nx, nz), out_shape=[jax.ShapeDty...  100 us
    unnamed x24, local copies, waits for them, and re-layouts  11.9 us

profile of v1, /device:TPU:1, one launch (start us, length us, event | category | flops | bytes accessed | tf_op | source)
XLA Modules:
  0.0 112.6 jit_solution(6900884976358487319)
XLA Ops:
  0.6 0.0 copy-start
  0.6 1.2 %copy-done = bf16[1,8,16,3584]{3,2,1,0:T(8,128)(2,1)S(1)} copy-done((bf16[1,8,16,3584]{3,2,1,0:T(8,128)(2,1)S(1)}, bf16[1,8,16,3584]{3,2,1,0:T(8,128)(2,1)}, u32[]{:S(2)}) %copy-start) | copy-done | bytes 917528
  1.8 0.0 copy-start.1
  1.8 0.9 copy-done.1
  2.8 0.0 copy-start.2
  2.8 0.9 copy-done.2
  3.7 0.0 copy-start.3
  3.7 0.9 copy-done.3
  4.7 0.0 copy-start.4
  4.7 0.9 copy-done.4
  5.6 0.0 copy-start.5
  5.6 0.9 copy-done.5
  6.5 0.0 copy-start.6
  6.5 0.7 copy-done.6
  7.2 0.0 copy-start.7
  7.2 0.7 copy-done.7
  7.9 100.0 %shard_map.127 = (bf16[512,256]{1,0:T(8,128)(2,1)S(1)}, bf16[512,256]{1,0:T(8,128)(2,1)S(1)}, f32[224,256]{1,0:T(8,128)S(1)}, f32[224,256]{1,0:T(8,128)S(1)}, f3...) custom-call(bf16[8,16,3584]{2,1,0:T(8,128)(2,1)S(1)} %bitcast.7, f32[8,16]{1,0:T(8,128)S(1)} %bitcast.12, ...), custom_call_target="tpu_custom_call" | custom-call | tf_op jit(solution)/shard_map/pallas_call | solution.py:541
  107.9 0.0 copy-start.8
  107.9 0.7 copy.20
  108.6 0.7 copy.21
  109.4 0.7 copy.22
  110.0 0.7 copy.23
  110.7 0.7 copy.24
  111.4 0.0 copy-done.8
  111.4 1.2 %copy.25 = bf16[3584,256]{1,0:T(8,128)(2,1)} copy(bf16[3584,256]{1,0:T(8,128)(2,1)S(1)} %bitcast.13) | data formatting | bytes 3670016
Async XLA Ops:
  0.6 1.2 %copy-start = (bf16[1,8,16,3584]{3,2,1,0:T(8,128)(2,1)S(1)}, bf16[1,8,16,3584]{3,2,1,0:T(8,128)(2,1)}, u32[]{:S(2)}) copy-start(bf16[1,8,16,3584]{3,2,1,0:T(8,128)(2,1)} %param.8) | copy-start | bytes 2752516
  1.8 0.9 copy-start.1
  2.8 0.9 copy-start.2
  3.7 0.9 copy-start.3
  4.7 0.9 copy-start.4
  5.6 0.9 copy-start.5
  6.5 0.7 copy-start.6
  7.2 0.7 copy-start.7
  107.9 3.5 %copy-start.8 = (bf16[8,2,224,256]{3,2,1,0:T(8,128)(2,1)S(1)}, bf16[8,2,224,256]{3,2,1,0:T(8,128)(2,1)}, u32[]{:S(2)}) copy-start(bf16[8,2,224,256]{3,2,1,0:T(8,128)(2,1)} %get-tuple-element.17) | copy-start | bytes 5505028

commit v2 on v0

v2 whole, which is shorter than its diff:
```python
import functools

import jax
import jax.numpy as jnp
from jax import lax
from jax.experimental import pallas as pl
from jax.experimental.pallas import tpu as pltpu
from jax.sharding import PartitionSpec as P

UNITS = (2, 2, 2, 1)
BEGIN = (0, 0, 0, 0)
STRIP = 32

learning_rate = 0.01
beta_one = 0.9
beta_two = 0.95
decay_rate = 0.1
epsilon = 1e-08

MESH = pl.DeviceIdType.MESH
BF16 = jnp.bfloat16
F32 = jnp.float32


def step_size(near, k):
    return (near - k) // 2 + 2


def step_start(near, k):
    return sum(step_size(near, j) for j in range(1, k))


def kernel(
    nx,
    nz,
    rows_hbm,
    weight_hbm,
    count_hbm,
    gate_hbm,
    up_hbm,
    master_hbm,
    first_hbm,
    second_hbm,
    dgate_ref,
    dup_ref,
    newm_ref,
    newf_ref,
    news_ref,
    fresh_ref,
    *scratch,
):
    chunks = len(UNITS)
    (
        outward,
        halves,
        origin,
        ring,
        last,
        columns,
        part,
        gsend,
        grecv,
        summed,
        across,
        row_sum,
        pieces,
    ) = (scratch[k * chunks : (k + 1) * chunks] for k in range(13))
    (
        rows_ref,
        weight_ref,
        count_ref,
        gate_ref,
        up_ref,
        master_ref,
        first_ref,
        second_ref,
        in_s,
        scaled,
        wown,
        wfull,
        hid,
        total,
        dh_out,
        dh_in,
        ys_s,
        yr_s,
        zs_s,
        zr_s,
        ws_s,
        wr_s,
        pair_s,
        gs_s,
        gr_s,
        xs_s,
        xr_s,
        ps_s,
        pr_s,
        as_s,
        ar_s,
        cs_s,
        cr_s,
    ) = scratch[13 * chunks :]
    flight, slots, width = rows_ref.shape
    shard, cols = master_ref.shape
    half = width // 2
    near = nz // 2
    low = slots // 2

    i, ez = lax.axis_index("dp"), lax.axis_index("expert")
    c, x, yh = lax.rem(i, 2), lax.rem(lax.div(i, 2), nx), lax.div(i, 2 * nx)
    z, yl = lax.div(ez, 2), lax.rem(ez, 2)
    zl, own_expert = lax.rem(z, 2), lax.div(z, 2)
    sibling = {"dp": i + 1 - 2 * c}
    z_pair = {"expert": ez + 2 - 4 * zl}
    y_pair = {"expert": ez + 1 - 2 * yl}
    y_across = {"dp": i + (1 - 2 * yh) * 2 * nx}
    z_next = (
        {"expert": lax.rem(z + 1, nz) * 2 + yl},
        {"expert": lax.rem(z + nz - 1, nz) * 2 + yl},
    )

    def dp_of(yh_, x_):
        return yh_ * (2 * nx) + x_ * 2 + c

    def x_next(step):
        return {"dp": dp_of(yh, lax.rem(x + step, nx))}

    def remote(src, dst, s, r, to):
        return pltpu.make_async_remote_copy(
            src_ref=src, dst_ref=dst, send_sem=s, recv_sem=r, device_id=to, device_id_type=MESH
        )

    loads = [
        pltpu.make_async_copy(src, dst, in_s.at[k])
        for k, (src, dst) in enumerate(
            (
                (rows_hbm, rows_ref),
                (weight_hbm, weight_ref),
                (count_hbm, count_ref),
                (master_hbm, master_ref),
                (gate_hbm, gate_ref),
                (up_hbm, up_ref),
                (first_hbm, first_ref),
                (second_hbm, second_ref),
            )
        )
    ]
    for load in loads:
        load.start()

    barrier = pltpu.get_barrier_semaphore()

    def greet(to):
        pl.semaphore_signal(barrier, inc=1, device_id=to, device_id_type=MESH)

    greet(z_next[0])
    greet(z_next[1])
    greet(sibling)

    greet(y_pair)
    greet(y_across)
    greet({"dp": dp_of(1 - yh, x), "expert": ez + 1 - 2 * yl})
    for step in range(1, nx):
        greet(x_next(step))

    for load in loads[:3]:
        load.wait()
    eye = lax.broadcasted_iota(jnp.int32, (slots, slots), 0) == lax.broadcasted_iota(
        jnp.int32, (slots, slots), 1
    )
    slot_of = lax.broadcasted_iota(jnp.int32, (slots, 1), 0)
    for e in range(flight):
        factor = jnp.sum(
            jnp.where(eye, jnp.broadcast_to(weight_ref[e : e + 1, :], (slots, slots)), 0.0),
            axis=1,
            keepdims=True,
        )
        factor = jnp.where(slot_of < count_ref[:, e : e + 1], factor, 0.0)
        block = rows_ref[e].astype(F32) * factor
        for h in range(2):
            side = block[:, h * half : (h + 1) * half]
            scaled[h, e] = side[:low]
            if e:
                scaled[h, flight] += side[low:]
            else:
                scaled[h, flight] = side[low:]
    expert_of = lax.broadcasted_iota(jnp.int32, (1, flight), 1)
    hot = jnp.max(
        jnp.where(jnp.logical_and(expert_of == own_expert, count_ref[...] > low), 1.0, 0.0),
        axis=1,
        keepdims=True,
    )

    group = lax.div(lax.broadcasted_iota(jnp.int32, (1, low, 128), 2), STRIP)
    per_tile = 128 // STRIP

    def pack(m, h, store):
        units, start = UNITS[m], sum(UNITS[:m])
        tiles = 2 * nx * units * STRIP // 128

        def gathered(tile):
            out = None
            for a in range(per_tile):
                owner, strip = divmod(tile * per_tile + a, units)
                at = owner * shard + (start + strip) * STRIP
                base, off = at // 128 * 128, at % 128
                moved = scaled[h, :, :, base : base + 128]
                shift = (a * STRIP - off) % 128
                if shift:
                    moved = pltpu.roll(moved, shift, 2)
                out = moved if out is None else jnp.where(group == a, moved, out)
            return out

        for tile in range(tiles // 2):
            both = jnp.concatenate([gathered(tile), gathered(tile + tiles // 2)], axis=1)
            store(slice(tile * 128, (tile + 1) * 128), both.astype(BF16))

    def pack_both(m):
        def to_outward(at, value):
            outward[m][:, :, at] = value

        def to_own(at, value):
            halves[m][yl, :, :, at] = value

        pack(m, 1 - yl, to_outward)
        pack(m, yl, to_own)

    def y_copy(m):
        return remote(outward[m], halves[m].at[yl], ys_s.at[m], yr_s.at[m], y_pair)

    def y_arrived(m):
        remote(outward[m], halves[m].at[1 - yl], ys_s.at[m], yr_s.at[m], y_pair).wait_recv()

    def combine(m):
        span = origin[m].shape[-1]

        def join(b):
            one, two = halves[m][0, b].astype(F32), halves[m][1, b].astype(F32)
            return (
                jnp.concatenate([one[:low], two[:low]], axis=0).astype(BF16),
                jnp.concatenate([one[low:], two[low:]], axis=0).astype(BF16),
            )

        left, right = join(flight)
        for d in range(2):
            origin[m][d, 0, :, : span // 2] = left
            origin[m][d, 0, :, span // 2 :] = right
        columns[m][1, z, :, : span // 2] = left
        columns[m][1, z, :, span // 2 :] = right
        for q in range(near // 2):
            for d in range(2):
                if d == 0:
                    e = lax.rem(own_expert + near // 2 - 1 + zl - q, flight)
                else:
                    e = lax.rem(own_expert + flight - near // 2 + zl + q, flight)
                left, right = join(e)
                origin[m][d, 1 + q, :, : span // 2] = left
                origin[m][d, 1 + q, :, span // 2 :] = right
        left, right = join(own_expert)
        columns[m][0, z, :, : span // 2] = left
        columns[m][0, z, :, span // 2 :] = right

    def ring_at(m, d, k):
        at = step_start(near, k)
        return ring[m].at[d, at : at + step_size(near, k)]

    def ring_copy(m, d, k):
        size = step_size(near, k)
        src = origin[m].at[d, :size] if k == 1 else ring_at(m, d, k - 1).at[:size]
        return remote(
            src, ring_at(m, d, k), zs_s.at[m, d, k - 1], zr_s.at[m, d, k - 1], z_next[d]
        )

    def last_copy(m):
        at = step_start(near, near - 1)
        return remote(
            ring[m].at[zl, at : at + step_size(near, near)],
            last[m],
            zs_s.at[m, 0, near - 1],
            zr_s.at[m, 0, near - 1],
            z_pair,
        )

    def ring_begin(m):
        y_arrived(m)
        combine(m)
        for d in range(2):
            ring_copy(m, d, 1).start()

    def ring_step(m, k):
        if k == near:
            last_copy(m).wait_recv()
            far = lax.rem(z + near, nz)
            columns[m][0, far] = last[m][1]
            columns[m][1, far] = last[m][0]
            return
        for d in range(2):
            ring_copy(m, d, k).wait_recv()
            if k + 1 < near:
                ring_copy(m, d, k + 1).start()
        if k + 1 == near:
            last_copy(m).start()
        for d in range(2):
            source = lax.rem(z + (nz - k if d == 0 else k), nz)
            base = step_start(near, k)
            keep = base + step_size(near, k) - 1
            if k % 2 == 0:
                keep = keep - (1 - zl if d == 0 else zl)
            columns[m][0, source] = ring[m][d, keep]
            columns[m][1, source] = ring[m][d, base]

    def weights_out(yh_):
        return (
            jnp.logical_and(yh_ == yh, yl == yh),
            remote(
                wown,
                wfull.at[yl, x, c],
                ws_s.at[yh_],
                wr_s.at[yl],
                {"dp": dp_of(yh_, x), "expert": z * 2 + yh},
            ),
        )

    def weights_in(yl_):
        return remote(wown, wfull.at[yl_, x, c], ws_s.at[0], wr_s.at[yl_], y_pair)

    def weights_along(step):
        slot = wfull.at[:, x, c]
        return remote(slot, slot, ws_s.at[1 + step], wr_s.at[1 + step], x_next(step))

    def weights_along_in(step):
        slot = wfull.at[:, lax.rem(x + nx - step, nx), c]
        return remote(slot, slot, ws_s.at[1 + step], wr_s.at[1 + step], sibling)

    def weights_over(core):
        slot = wfull.at[:, :, core]
        return remote(slot, slot, ws_s.at[1 + nx], wr_s.at[1 + nx], sibling)

    def send_weights():
        loads[3].wait()
        wown[...] = master_ref[...].astype(BF16)
        for yh_ in range(2):
            own, copy = weights_out(yh_)

            @pl.when(jnp.logical_not(own))
            def _(copy=copy):
                copy.start()

            @pl.when(own)
            def _():
                pltpu.make_async_copy(wown, wfull.at[yl, x, c], wr_s.at[yl]).start()

    def pass_weights():
        for yl_ in range(2):
            weights_in(yl_).wait_recv()
        for step in range(1, nx):
            weights_along(step).start()

    def share_weights():
        for step in range(1, nx):
            weights_along_in(step).wait_recv()
        weights_over(c).start()

    def weights_sent():
        for yh_ in range(2):
            own, copy = weights_out(yh_)

            @pl.when(jnp.logical_not(own))
            def _(copy=copy):
                copy.wait_send()

        for step in range(1, nx):
            weights_along(step).wait_send()
        weights_over(c).wait_send()

    def swish(k, carry):
        at = pl.ds(pl.multiple_of(k * 2 * slots, 2 * slots), 2 * slots)
        to = pl.ds(pl.multiple_of(k * slots, slots), slots)
        gate = gate_ref[at, :].astype(F32)
        up = up_ref[at, :].astype(F32)
        value = gate * jax.nn.sigmoid(gate) * up
        hid[yl, 0, to, :] = jnp.concatenate([value[:low], value[slots : slots + low]], 0).astype(
            BF16
        )
        extra = jnp.concatenate([value[low:slots], value[slots + low :]], 0)
        hid[yl, 1, to, :] = (extra * hot).astype(BF16)
        return carry

    hid_copy = remote(hid.at[yl], hid.at[yl], pair_s.at[0], pair_s.at[1], y_pair)

    def send_hidden():
        loads[4].wait()
        loads[5].wait()
        lax.fori_loop(0, nz, swish, 0)
        hid_copy.start()

    def hidden_arrived():
        remote(hid.at[yl], hid.at[1 - yl], pair_s.at[0], pair_s.at[1], y_pair).wait_recv()

    starts = [sum(UNITS[:m]) * STRIP for m in range(chunks)]
    counts = [units * STRIP for units in UNITS]

    def to_sibling(m):
        return remote(gsend[m], grecv[m], gs_s.at[m], gr_s.at[m], sibling)

    def columns_of(m):
        return columns[m][...].reshape(2 * nz * slots, columns[m].shape[-1])

    def gradient(m):
        for y_ in range(2):
            part[m][y_] = lax.dot_general(
                columns_of(m), hid[y_].reshape(-1, cols), (((0,), (0,)), ((), ())), preferred_element_type=F32
            ).reshape(nx, 2, counts[m], cols)
        gsend[m][...] = part[m][:, :, 1 - c].astype(BF16)
        to_sibling(m).start()

    def back(m):
        for y_ in range(2):
            block = wfull[y_, :, :, starts[m] : starts[m] + counts[m], :].reshape(-1, cols)
            product = jnp.dot(columns_of(m), block, preferred_element_type=F32)
            if m:
                total[y_] += product
            else:
                total[y_] = product

    def along_copy(m, step):
        return remote(
            summed[m].at[:, lax.rem(x + step, nx)],
            across[m].at[step - 1],
            xs_s.at[m, step - 1],
            xr_s.at[m, step - 1],
            x_next(step),
        )

    def piece_copy(m, y_):
        own = jnp.logical_and(yh == yl, yl == y_)
        src, dst, sem = row_sum[m].at[y_], pieces[m].at[yh], pr_s.at[m, yh]
        to = {"dp": dp_of(yl, x), "expert": z * 2 + y_}
        return own, remote(src, dst, ps_s.at[m, y_], sem, to), (src, dst, sem)

    def reduce_cores(m):
        to_sibling(m).wait_recv()
        summed[m][...] = (part[m][:, :, c] + grecv[m][...].astype(F32)).astype(BF16)
        for step in range(1, nx):
            along_copy(m, step).start()

    def reduce_along(m):
        for step in range(1, nx):
            along_copy(m, step).wait_recv()
        value = summed[m][:, x].astype(F32)
        for step in range(1, nx):
            value += across[m][step - 1].astype(F32)
        row_sum[m][...] = value.astype(BF16)
        for y_ in range(2):
            own, copy, local = piece_copy(m, y_)

            @pl.when(jnp.logical_not(own))
            def _(copy=copy):
                copy.start()

            @pl.when(own)
            def _(local=local):
                pltpu.make_async_copy(*local).start()

    def rows_of(m):
        return pl.ds(starts[m], counts[m])

    def fresh_across(m, yh_):
        slot = fresh_ref.at[yh_, x, c, rows_of(m)]
        return remote(slot, slot, as_s.at[m, 0], ar_s.at[m, 0], y_across)

    def fresh_along(m, step, x_):
        slot = fresh_ref.at[:, x_, c, rows_of(m)]
        return remote(slot, slot, as_s.at[m, step], ar_s.at[m, step], x_next(step))

    def fresh_over(m, core):
        slot = fresh_ref.at[:, :, core, rows_of(m)]
        return remote(slot, slot, cs_s.at[m], cr_s.at[m], sibling)

    def update(m):
        for yh_ in range(2):
            remote(
                row_sum[m].at[0], pieces[m].at[yh_], ps_s.at[m, 0], pr_s.at[m, yh_], sibling
            ).wait_recv()
        at = slice(starts[m], starts[m] + counts[m])
        grad = pieces[m][0].astype(F32) + pieces[m][1].astype(F32)
        master = master_ref[at, :]
        moment_a = beta_one * first_ref[at, :] + (1.0 - beta_one) * grad
        moment_b = beta_two * second_ref[at, :] + (1.0 - beta_two) * grad * grad
        step = (
            moment_a
            / (1.0 - beta_one**5)
            / (jnp.sqrt(moment_b / (1.0 - beta_two**5)) + epsilon)
        )
        updated = master - learning_rate * (step + decay_rate * master)
        fresh_ref[yh, x, c, at, :] = updated.astype(BF16)
        fresh_across(m, yh).start()
        newm_ref[at, :] = updated
        newf_ref[at, :] = moment_a
        news_ref[at, :] = moment_b

    def gather_along(m):
        fresh_across(m, 1 - yh).wait_recv()
        for step in range(1, nx):
            fresh_along(m, step, x).start()

    def gather_over(m):
        for step in range(1, nx):
            fresh_along(m, step, lax.rem(x + nx - step, nx)).wait_recv()
        fresh_over(m, c).start()

    dh_copy = remote(dh_out, dh_in, pair_s.at[2], pair_s.at[3], y_pair)

    def finish_hidden():
        dh_copy.wait_recv()

        def one(k, carry):
            at = pl.ds(pl.multiple_of(k * 2 * slots, 2 * slots), 2 * slots)
            base = pl.ds(pl.multiple_of(k * slots, slots), slots)
            extra = pl.ds(pl.multiple_of((nz + k) * slots, slots), slots)
            gate = gate_ref[at, :].astype(F32)
            up = up_ref[at, :].astype(F32)
            sig = jax.nn.sigmoid(gate)
            low_rows = total[yl, base, :] + dh_in[base, :].astype(F32)
            high_rows = (total[yl, extra, :] + dh_in[extra, :].astype(F32)) * hot
            dh = jnp.concatenate(
                [low_rows[:low], high_rows[:low], low_rows[low:], high_rows[low:]], axis=0
            )
            dgate_ref[at, :] = (dh * up * sig * (1.0 + gate * (1.0 - sig))).astype(BF16)
            dup_ref[at, :] = (dh * (gate * sig)).astype(BF16)
            return carry

        lax.fori_loop(0, nz, one, 0)

    def products(m):
        gradient(m)
        back(m)
        if m == chunks - 1:
            dh_out[...] = total[1 - yl].astype(BF16)
            dh_copy.start()

    stages = (products, reduce_cores, reduce_along, update, gather_along, gather_over)

    def beat(tick):
        for m in range(chunks):
            stage = tick - BEGIN[m] - near
            if 0 <= stage < len(stages):
                stages[stage](m)

    pack_both(0)
    pl.semaphore_wait(barrier, nx + 5)
    y_copy(0).start()
    for m in range(1, chunks):
        pack_both(m)
        y_copy(m).start()
    for tick in range(BEGIN[-1] + near + 1):
        for m in range(chunks):
            k = tick - BEGIN[m]
            if k == 0:
                ring_begin(m)
            elif 1 <= k <= near:
                ring_step(m, k)
        if tick == 0:
            send_weights()
            send_hidden()
        if tick == 2:
            pass_weights()
        if tick == near - 2:
            share_weights()
        if tick == near:
            hidden_arrived()
            loads[6].wait()
            loads[7].wait()
            weights_over(1 - c).wait_recv()
        beat(tick)
    for m in range(chunks):
        y_copy(m).wait_send()
        for k in range(1, near):
            for d in range(2):
                ring_copy(m, d, k).wait_send()
        last_copy(m).wait_send()
    weights_sent()
    hid_copy.wait_send()
    for tick in range(BEGIN[-1] + near + 1, BEGIN[-1] + near + 6):
        beat(tick)
        if tick == BEGIN[-1] + near + 2:
            finish_hidden()
    dh_copy.wait_send()
    for m in range(chunks):
        to_sibling(m).wait_send()
        for step in range(1, nx):
            along_copy(m, step).wait_send()
        for y_ in range(2):
            own, copy, _ = piece_copy(m, y_)

            @pl.when(jnp.logical_not(own))
            def _(copy=copy):
                copy.wait_send()

        fresh_across(m, yh).wait_send()
        for step in range(1, nx):
            fresh_along(m, step, x).wait_send()
        fresh_over(m, c).wait_send()
        fresh_over(m, 1 - c).wait_recv()


def hand_over(*refs):
    count = (len(refs) - 2) // 3
    sources, results, held = (refs[k * count : (k + 1) * count] for k in range(3))
    in_s, out_s = refs[-2:]
    loads = [
        pltpu.make_async_copy(sources[k], held[k], in_s.at[k]) for k in range(count)
    ]
    stores = [
        pltpu.make_async_copy(held[k], results[k], out_s.at[k]) for k in range(count)
    ]
    for load in loads:
        load.start()
    for load, store in zip(loads, stores):
        load.wait()
        store.start()
    for store in stores:
        store.wait()


def local(nx, nz, rows, weight, count, gate, up, master, first, second):
    _, flight, slots, width = rows.shape
    shard, cols = master.shape
    _, received, _ = gate.shape
    chunks = len(UNITS)
    counts = [units * STRIP for units in UNITS]
    assert sum(counts) == shard and cols % 128 == 0
    spans = [2 * nx * n for n in counts]
    vmem = pl.BlockSpec(memory_space=pltpu.VMEM)
    dma = pltpu.SemaphoreType.DMA
    near = nz // 2
    blocks = step_start(near, near)
    hbm = pl.BlockSpec(memory_space=pltpu.HBM)
    scratch = (
        [pltpu.VMEM((flight + 1, slots, n // 2), BF16) for n in spans]
        + [pltpu.VMEM((2, flight + 1, slots, n // 2), BF16) for n in spans]
        + [pltpu.VMEM((2, near // 2 + 1, slots, n), BF16) for n in spans]
        + [pltpu.VMEM((2, blocks, slots, n), BF16) for n in spans]
        + [pltpu.VMEM((step_size(near, near), slots, n), BF16) for n in spans]
        + [pltpu.VMEM((2, nz, slots, n), BF16) for n in spans]
        + [pltpu.VMEM((2, nx, 2, n, cols), F32) for n in counts]
        + [pltpu.VMEM((2, nx, n, cols), BF16) for n in counts]
        + [pltpu.VMEM((2, nx, n, cols), BF16) for n in counts]
        + [pltpu.VMEM((2, nx, n, cols), BF16) for n in counts]
        + [pltpu.VMEM((nx - 1, 2, n, cols), BF16) for n in counts]
        + [pltpu.VMEM((2, n, cols), BF16) for n in counts]
        + [pltpu.VMEM((2, n, cols), BF16) for n in counts]
        + [
            pltpu.VMEM((flight, slots, width), BF16),
            pltpu.VMEM((flight, slots), F32),
            pltpu.VMEM((1, flight), jnp.int32),
            pltpu.VMEM((received, cols), BF16),
            pltpu.VMEM((received, cols), BF16),
            pltpu.VMEM((shard, cols), F32),
            pltpu.VMEM((shard, cols), F32),
            pltpu.VMEM((shard, cols), F32),
            dma((8,)),
            pltpu.VMEM((2, flight + 1, slots // 2, width // 2), F32),
            pltpu.VMEM((shard, cols), BF16),
            pltpu.VMEM((2, nx, 2, shard, cols), BF16),
            pltpu.VMEM((2, 2, received // 2, cols), BF16),
            pltpu.VMEM((2, received, cols), F32),
            pltpu.VMEM((received, cols), BF16),
            pltpu.VMEM((received, cols), BF16),
            dma((chunks,)),
            dma((chunks,)),
            dma((chunks, 2, near)),
            dma((chunks, 2, near)),
            dma((nx + 2,)),
            dma((nx + 2,)),
            dma((4,)),
            dma((chunks,)),
            dma((chunks,)),
            dma((chunks, nx - 1)),
            dma((chunks, nx - 1)),
            dma((chunks, 2)),
            dma((chunks, 2)),
            dma((chunks, nx)),
            dma((chunks, nx)),
            dma((chunks,)),
            dma((chunks,)),
        ]
    )
    outs = pl.pallas_call(
        functools.partial(kernel, nx, nz),
        out_shape=[
            jax.ShapeDtypeStruct((received, cols), BF16),
            jax.ShapeDtypeStruct((received, cols), BF16),
            jax.ShapeDtypeStruct((shard, cols), F32),
            jax.ShapeDtypeStruct((shard, cols), F32),
            jax.ShapeDtypeStruct((shard, cols), F32),
            jax.ShapeDtypeStruct((2, nx, 2, shard, cols), BF16),
        ],
        in_specs=[hbm] * 8,
        out_specs=[vmem] * 6,
        scratch_shapes=scratch,
        compiler_params=pltpu.CompilerParams(
            collective_id=0, has_side_effects=True, vmem_limit_bytes=62 * 1024 * 1024
        ),
    )(rows[0], weight[0], count, gate[0], up[0], master, first, second)
    outs = pl.pallas_call(
        hand_over,
        out_shape=[jax.ShapeDtypeStruct(o.shape, o.dtype) for o in outs],
        in_specs=[hbm] * 6,
        out_specs=[hbm] * 6,
        scratch_shapes=[pltpu.VMEM(o.shape, o.dtype) for o in outs] + [dma((6,)), dma((6,))],
        compiler_params=pltpu.CompilerParams(vmem_limit_bytes=62 * 1024 * 1024),
    )(*outs)
    return (
        outs[0][None],
        outs[1][None],
        outs[2],
        outs[3],
        outs[4],
        outs[5].reshape(4 * nx * shard, cols),
    )


def solution(mesh):
    nx, nz = mesh.shape["dp"] // 4, mesh.shape["expert"] // 2
    placed = (
        P("dp", "expert", None, None),
        P("dp", "expert", None),
        P("dp", "expert"),
        P("dp", None, "expert"),
        P("dp", None, "expert"),
        P("dp", "expert"),
        P("dp", "expert"),
        P("dp", "expert"),
    )
    return jax.shard_map(
        functools.partial(local, nx, nz),
        mesh=mesh,
        in_specs=placed,
        out_specs=(
            P("dp", None, "expert"),
            P("dp", None, "expert"),
            P("dp", "expert"),
            P("dp", "expert"),
            P("dp", "expert"),
            P(None, "expert"),
        ),
        check_vma=False,
    )
```

time: 427 us -> 94.6 us (0.22)
  waiting for transfers between devices: 214 us -> 0 us
  blocking collectives: 183 us -> 0 us
  Pallas kernels: 0 us -> 93.7 us
  between operations: 13.8 us -> 0.64 us
  matrix products: 7.1 us -> 0 us
  local copies, waits for them, and re-layouts: 5.1 us -> 0 us
    all_to_all x1 -> x0, blocking collectives: 183 us -> none  [local(): lax.all_to_all(spread, 'expert', split_axis=0, concat_axis=0, tiled=True)]
    all_gather x2 -> x0, waiting for transfers between devices: 128 us -> none  [the longest x1 66.2 us: local(): lax.all_gather(master_weight.astype(jnp.bfloat16), 'dp', axis=0, tiled=True)]
    pallas_call x0 -> x2, Pallas kernels: none -> 93.7 us  [the longest x1 90.5 us: local(): pl.pallas_call(functools.partial(kernel, nx, nz), out_shape=[jax.ShapeDty...]
    reduce_scatter x1 -> x0, waiting for transfers between devices: 85.5 us -> none  [local(): lax.psum_scatter(lax.dot_general(columns, hidden, (((0,), (0,)), ((), ())...]
    dot_general x2 -> x0, matrix products: 7.1 us -> none  [the longest x1 4.59 us: local(): jnp.dot(columns, lax.all_gather(master_weight.astype(jnp.bfloat16), 'dp',...]
    unnamed x13 -> x0, local copies, waits for them, and re-layouts: 4.67 us -> none
  transfers between devices with their start and end apart: 3 -> 0, of which waited for: 3 -> 0; matrix products, arithmetic and copies ran while one was open for 1% -> 0% of each run, Pallas kernels for 0% -> 0%
where the time goes in v2:
time: 94.6 us; the launch traced here: 94.4 us
  Pallas kernels  93.7 us (99%)
    pallas_call x1, Pallas kernels, local(): pl.pallas_call(functools.partial(kernel, nx, nz), out_shape=[jax.ShapeDty...  90.5 us
    pallas_call x1, Pallas kernels, local(): pl.pallas_call(hand_over, out_shape=[jax.ShapeDtypeStruct(o.shape, o.dtyp...  3.22 us

profile of v2, /device:TPU:1, one launch (start us, length us, event | category | flops | bytes accessed | tf_op | source)
XLA Modules:
  0.0 94.4 jit_solution(2082154092531817918)
XLA Ops:
  0.6 90.5 %shard_map.127 = (bf16[512,256]{1,0:T(8,128)(2,1)}, bf16[512,256]{1,0:T(8,128)(2,1)}, f32[224,256]{1,0:T(8,128)}, f32[224,256]{1,0:T(8,128)}, f32[224,256]{1,0:T(8,128)}, /*index=5*/bf16[2,4,2,224,256]{4,3,2,1,0:T(8,128)(2,1)}) custom-call(bf16[8,16,3584]{2,1,0:T(8,128)(2,1)} %bitcast.7, f32[8,16]{1,0:T(8,128)} %bitcast.10, s32[1,8]{1,0:T(1,128)} %count_hbm.1, ...), custom_call_target="tpu_custom_call" | custom-call | tf_op jit(solution)/shard_map/pallas_call | solution.py:689
  91.2 3.2 %shard_map.128 = (bf16[512,256]{1,0:T(8,128)(2,1)}, bf16[512,256]{1,0:T(8,128)(2,1)}, f32[224,256]{1,0:T(8,128)}, f32[224,256]{1,0:T(8,128)}, f32[224,256]{1,0:T(8,128)}, /*index=5*/bf16[2,4,2,224,256]{4,3,2,1,0:T(8,128)(2,1)}) custom-call(bf16[512,256]{1,0:T(8,128)(2,1)} %get-tuple-element.18.refs_0_, bf16[512,256]{1,0:T(8,128)(2,1)} %get-tuple-element.19.refs_1_, ...), custom_call_target="tpu_custom_call" | custom-call | tf_op jit(solution)/shard_map/pallas_call | solution.py:706

commit v3 on v2

--- a/solution.py
+++ b/solution.py
@@ -8,7 +8,6 @@
 from jax.sharding import PartitionSpec as P
 
 UNITS = (2, 2, 2, 1)
-BEGIN = (0, 0, 0, 0)
 STRIP = 32
 
 learning_rate = 0.01
@@ -215,15 +214,17 @@
             both = jnp.concatenate([gathered(tile), gathered(tile + tiles // 2)], axis=1)
             store(slice(tile * 128, (tile + 1) * 128), both.astype(BF16))
 
-    def pack_both(m):
-        def to_outward(at, value):
+    def pack_outward(m):
+        def store(at, value):
             outward[m][:, :, at] = value
 
-        def to_own(at, value):
+        pack(m, 1 - yl, store)
+
+    def pack_own(m):
+        def store(at, value):
             halves[m][yl, :, :, at] = value
 
-        pack(m, 1 - yl, to_outward)
-        pack(m, yl, to_own)
+        pack(m, yl, store)
 
     def y_copy(m):
         return remote(outward[m], halves[m].at[yl], ys_s.at[m], yr_s.at[m], y_pair)
@@ -231,34 +232,30 @@
     def y_arrived(m):
         remote(outward[m], halves[m].at[1 - yl], ys_s.at[m], yr_s.at[m], y_pair).wait_recv()
 
-    def combine(m):
+    def join(m, b):
+        one, two = halves[m][0, b].astype(F32), halves[m][1, b].astype(F32)
+        return (
+            jnp.concatenate([one[:low], two[:low]], axis=0).astype(BF16),
+            jnp.concatenate([one[low:], two[low:]], axis=0).astype(BF16),
+        )
+
+    def combine(m, d):
         span = origin[m].shape[-1]
-
-        def join(b):
-            one, two = halves[m][0, b].astype(F32), halves[m][1, b].astype(F32)
-            return (
-                jnp.concatenate([one[:low], two[:low]], axis=0).astype(BF16),
-                jnp.concatenate([one[low:], two[low:]], axis=0).astype(BF16),
-            )
-
-        left, right = join(flight)
-        for d in range(2):
-            origin[m][d, 0, :, : span // 2] = left
-            origin[m][d, 0, :, span // 2 :] = right
-        columns[m][1, z, :, : span // 2] = left
-        columns[m][1, z, :, span // 2 :] = right
+        left, right = join(m, flight)
+        origin[m][d, 0, :, : span // 2] = left
+        origin[m][d, 0, :, span // 2 :] = right
         for q in range(near // 2):
-            for d in range(2):
-                if d == 0:
-                    e = lax.rem(own_expert + near // 2 - 1 + zl - q, flight)
-                else:
-                    e = lax.rem(own_expert + flight - near // 2 + zl + q, flight)
-                left, right = join(e)
-                origin[m][d, 1 + q, :, : span // 2] = left
-                origin[m][d, 1 + q, :, span // 2 :] = right
-        left, right = join(own_expert)
-        columns[m][0, z, :, : span // 2] = left
-        columns[m][0, z, :, span // 2 :] = right
+            if d == 0:
+                e = lax.rem(own_expert + near // 2 - 1 + zl - q, flight)
+            else:
+                e = lax.rem(own_expert + flight - near // 2 + zl + q, flight)
+            left, right = join(m, e)
+            origin[m][d, 1 + q, :, : span // 2] = left
+            origin[m][d, 1 + q, :, span // 2 :] = right
+
+    def keep_own(m):
+        columns[m][0, z] = origin[m][zl, near // 2]
+        columns[m][1, z] = origin[m][0, 0]
 
     def ring_at(m, d, k):
         at = step_start(near, k)
@@ -283,16 +280,13 @@
 
     def ring_begin(m):
         y_arrived(m)
-        combine(m)
         for d in range(2):
+            combine(m, d)
             ring_copy(m, d, 1).start()
 
-    def ring_step(m, k):
+    def ring_pass(m, k):
         if k == near:
             last_copy(m).wait_recv()
-            far = lax.rem(z + near, nz)
-            columns[m][0, far] = last[m][1]
-            columns[m][1, far] = last[m][0]
             return
         for d in range(2):
             ring_copy(m, d, k).wait_recv()
@@ -300,6 +294,13 @@
                 ring_copy(m, d, k + 1).start()
         if k + 1 == near:
             last_copy(m).start()
+
+    def ring_keep(m, k):
+        if k == near:
+            far = lax.rem(z + near, nz)
+            columns[m][0, far] = last[m][1]
+            columns[m][1, far] = last[m][0]
+            return
         for d in range(2):
             source = lax.rem(z + (nz - k if d == 0 else k), nz)
             base = step_start(near, k)
@@ -539,27 +540,37 @@
             dh_out[...] = total[1 - yl].astype(BF16)
             dh_copy.start()
 
-    stages = (products, reduce_cores, reduce_along, update, gather_along, gather_over)
-
-    def beat(tick):
-        for m in range(chunks):
-            stage = tick - BEGIN[m] - near
-            if 0 <= stage < len(stages):
-                stages[stage](m)
-
-    pack_both(0)
+    expected = (
+        (reduce_cores, 3.0, 0.3),
+        (reduce_along, 9.2, 2.7),
+        (update, 13.7, 2.7),
+        (gather_along, 17.7, 2.7),
+        (gather_over, 24.0, 3.0),
+    )
+    order = sorted(
+        (first + lag * m, at, m)
+        for at, (_, first, lag) in enumerate(expected)
+        for m in range(chunks)
+    )
+
+    pack_outward(0)
     pl.semaphore_wait(barrier, nx + 5)
     y_copy(0).start()
     for m in range(1, chunks):
-        pack_both(m)
+        pack_outward(m)
         y_copy(m).start()
-    for tick in range(BEGIN[-1] + near + 1):
-        for m in range(chunks):
-            k = tick - BEGIN[m]
-            if k == 0:
-                ring_begin(m)
-            elif 1 <= k <= near:
-                ring_step(m, k)
+    for m in range(chunks):
+        pack_own(m)
+        ring_begin(m)
+    for tick in range(near):
+        if tick:
+            for m in range(chunks):
+                ring_pass(m, tick)
+            for m in range(chunks):
+                ring_keep(m, tick)
+        else:
+            for m in range(chunks):
+                keep_own(m)
         if tick == 0:
             send_weights()
             send_hidden()
@@ -567,12 +578,21 @@
             pass_weights()
         if tick == near - 2:
             share_weights()
-        if tick == near:
+        if tick == near - 1:
             hidden_arrived()
             loads[6].wait()
             loads[7].wait()
             weights_over(1 - c).wait_recv()
-        beat(tick)
+    for m in range(chunks):
+        ring_pass(m, near)
+        ring_keep(m, near)
+        products(m)
+    hidden_done = False
+    for when, at, m in order:
+        if when > 16.2 and not hidden_done:
+            finish_hidden()
+            hidden_done = True
+        expected[at][0](m)
     for m in range(chunks):
         y_copy(m).wait_send()
         for k in range(1, near):
@@ -581,10 +601,6 @@
         last_copy(m).wait_send()
     weights_sent()
     hid_copy.wait_send()
-    for tick in range(BEGIN[-1] + near + 1, BEGIN[-1] + near + 6):
-        beat(tick)
-        if tick == BEGIN[-1] + near + 2:
-            finish_hidden()
     dh_copy.wait_send()
     for m in range(chunks):
         to_sibling(m).wait_send()

time: 94.6 us -> 91.5 us (0.967)
  Pallas kernels: 93.7 us -> 90.7 us
    pallas_call x1, Pallas kernels: 90.5 us -> 87.4 us  [local(): pl.pallas_call(functools.partial(kernel, nx, nz), out_shape=[jax.ShapeDty...]
where the time goes in v3:
time: 91.5 us; the launch traced here: 91.3 us
  Pallas kernels  90.7 us (99%)
    pallas_call x1, Pallas kernels, local(): pl.pallas_call(functools.partial(kernel, nx, nz), out_shape=[jax.ShapeDty...  87.4 us
    pallas_call x1, Pallas kernels, local(): pl.pallas_call(hand_over, out_shape=[jax.ShapeDtypeStruct(o.shape, o.dtyp...  3.22 us

profile of v3, /device:TPU:1, one launch (start us, length us, event | category | flops | bytes accessed | tf_op | source)
XLA Modules:
  0.0 91.3 jit_solution(4297788222965258192)
XLA Ops:
  0.6 87.4 %shard_map.127 = (bf16[512,256]{1,0:T(8,128)(2,1)}, bf16[512,256]{1,0:T(8,128)(2,1)}, f32[224,256]{1,0:T(8,128)}, f32[224,256]{1,0:T(8,128)}, f32[224,256]{1,0:T(8,128)}, /*index=5*/bf16[2,4,2,224,256]{4,3,2,1,0:T(8,128)(2,1)}) custom-call(bf16[8,16,3584]{2,1,0:T(8,128)(2,1)} %bitcast.7, f32[8,16]{1,0:T(8,128)} %bitcast.10, s32[1,8]{1,0:T(1,128)} %count_hbm.1, ...), custom_call_target="tpu_custom_call" | custom-call | tf_op jit(solution)/shard_map/pallas_call | solution.py:705
  88.1 3.2 %shard_map.128 = (bf16[512,256]{1,0:T(8,128)(2,1)}, bf16[512,256]{1,0:T(8,128)(2,1)}, f32[224,256]{1,0:T(8,128)}, f32[224,256]{1,0:T(8,128)}, f32[224,256]{1,0:T(8,128)}, /*index=5*/bf16[2,4,2,224,256]{4,3,2,1,0:T(8,128)(2,1)}) custom-call(bf16[512,256]{1,0:T(8,128)(2,1)} %get-tuple-element.18.refs_0_, bf16[512,256]{1,0:T(8,128)(2,1)} %get-tuple-element.19.refs_1_, ...), custom_call_target="tpu_custom_call" | custom-call | tf_op jit(solution)/shard_map/pallas_call | solution.py:722
